TPU v7x, 32 devices: a whole 2x2x4 slice. The times are simulated.
32 devices in a mesh: dp: 8 (over z, x), tensor: 4 (over y, core).
Axes of the slice: x: 2, y: 2, z: 4, core: 2. Of those that a mesh axis runs over, the one named last changes fastest.
Arguments:
- hidden_in: bfloat16 [8192, 1152], P(('dp', 'tensor')), may hold values from -6 to 6
- picture_ids: int32 [8192], P('dp'), may hold values from -1 to 9, as said below
- norm1_gain: float32 [1152], replicated, may hold values from 0.5 to 1.5
- norm1_bias: float32 [1152], replicated, may hold values from -1.75 to 1.75
- w_qkv: bfloat16 [3, 1152, 1152], P(None, None, 'tensor'), may hold values from -1 to 1
- qv_bias: float32 [2, 1152], P(None, 'tensor'), may hold values from -3 to 3
- w_out: bfloat16 [1152, 1152], P('tensor'), may hold values from -0.75 to 0.75
- out_bias: float32 [1152], replicated, may hold values from -1.75 to 1.75
- norm2_gain: float32 [1152], replicated, may hold values from 0.5 to 1.5
- norm2_bias: float32 [1152], replicated, may hold values from -1.75 to 1.75
- w_up: bfloat16 [1152, 4304], P(None, 'tensor'), may hold values from -0.1875 to 0.1875
- up_bias: float32 [4304], P('tensor'), may hold values from -3 to 3
- w_down: bfloat16 [4304, 1152], P('tensor'), may hold values from -0.125 to 0.125
- down_bias: float32 [1152], replicated, may hold values from -1.75 to 1.75
- cotangent: bfloat16 [8192, 1152], P(('dp', 'tensor')), may hold values from -6 to 6
Outputs:
- hidden_out: bfloat16 [8192, 1152], P(('dp', 'tensor'))
- grad_in: bfloat16 [8192, 1152], P(('dp', 'tensor'))
- grad_qkv: float32 [3, 1152, 1152], P(None, 'dp', 'tensor')
- grad_out: float32 [1152, 1152], P('tensor', 'dp')
- grad_up: float32 [1152, 4304], P('dp', 'tensor')
- grad_down: float32 [4304, 1152], P('tensor', 'dp')
- grad_qv_bias: float32 [2, 1152], P(None, 'tensor')
- grad_up_bias: float32 [4304], P('tensor')
- grad_shared: float32 [6, 1152], replicated
- head_maxima: float32 [16], P('tensor')
- scaled_qk: bfloat16 [2, 1152, 1152], P(None, None, 'tensor')
- scaled_query_bias: float32 [1152], P('tensor')
Inputs may be any that keep to these rules, and one draw needn't show every extreme that they name: `picture_ids`: each aligned row of 1024 tokens holds whole pictures of 100 to 1024 patches one after another, numbered from 0 within the row, then padding with id -1; some row holds a single picture of 1024 patches, and some other row holds 10 pictures of 100 patches.
All inputs are finite; a program needn't handle non-finite values.
Results may differ from a plain program's by a relative error of at most 0.014.
Values may be sent and summed in bfloat16 or wider, within the bound.
No kernel may reach another device: no remote copies, remote signals or barrier semaphores. Data moves between devices by JAX's collectives and lax.ppermute only.
A program may use at most 192 MiB of HBM per device.

v0:
```python
import jax
import jax.numpy as jnp
from jax import lax
from jax.sharding import PartitionSpec as P

HEAD_DIM = 72
PACK = 1024
QBLOCK = 512
CLIP_LIMIT = 9
eps_norm = 1e-06
neg_fill = -1e30


def normalize(values_in, gain, shift):
    row_mean = jnp.mean(values_in, axis=-1, keepdims=True)
    centred = values_in - row_mean
    variance = jnp.mean(centred * centred, axis=-1, keepdims=True)
    inverse = lax.rsqrt(variance + eps_norm)
    unit_rows = centred * inverse
    return (unit_rows * gain + shift, unit_rows, inverse)


def norm_back(grad_rows, unit_rows, inverse, gain):
    scaled = grad_rows * gain
    return inverse * (
        scaled
        - jnp.mean(scaled, axis=-1, keepdims=True)
        - unit_rows * jnp.mean(scaled * unit_rows, axis=-1, keepdims=True)
    )


def gelu_tanh(inputs):
    return jax.nn.gelu(inputs, approximate=True)


def local(
    hidden_in,
    picture_ids,
    norm1_gain,
    norm1_bias,
    w_qkv,
    qv_bias,
    w_out,
    out_bias,
    norm2_gain,
    norm2_bias,
    w_up,
    up_bias,
    w_down,
    down_bias,
    cotangent,
):
    group_rows = picture_ids.shape[0]
    row_count = group_rows // PACK
    head_width = w_qkv.shape[2]
    local_heads = head_width // HEAD_DIM
    score_scale = HEAD_DIM ** (-0.5)
    block_count = PACK // QBLOCK
    block_shape = (row_count, block_count, QBLOCK, local_heads, HEAD_DIM)
    row_shape = (row_count, PACK, local_heads, HEAD_DIM)
    source = hidden_in.astype(jnp.float32)
    normed_a, unit_a, inverse_a = normalize(source, norm1_gain, norm1_bias)
    whole_a = lax.all_gather(normed_a.astype(jnp.bfloat16), "tensor", axis=0, tiled=True)
    projected = jnp.einsum("td,cde->cte", whole_a, w_qkv, preferred_element_type=jnp.float32)
    queries = (projected[0] + qv_bias[0]).astype(jnp.bfloat16)
    key_rows = projected[1].astype(jnp.bfloat16)
    values = (projected[2] + qv_bias[1]).astype(jnp.bfloat16)
    query_blocks = queries.reshape(block_shape)
    key_heads = key_rows.reshape(row_shape)
    value_heads = values.reshape(row_shape)
    row_ids = picture_ids.reshape(row_count, PACK)

    def attend_row(parts_in):
        row_q, row_k, row_v, ids_row = parts_in
        block_ids = ids_row.reshape(block_count, QBLOCK)

        def attend_block(block_in):
            block_q, query_ids = block_in
            scores = (
                jnp.einsum("qhd,khd->hqk", block_q, row_k, preferred_element_type=jnp.float32)
                * score_scale
            )
            allowed = query_ids[:, None] == ids_row[None, :]
            scores = jnp.where(allowed[None], scores, neg_fill)
            row_top = jnp.max(scores, axis=2, keepdims=True)
            weights = jnp.exp(scores - row_top)
            row_sum = jnp.sum(weights, axis=2, keepdims=True)
            prob_rows = (weights / row_sum).astype(jnp.bfloat16)
            attended = jnp.einsum(
                "hqk,khd->qhd", prob_rows, row_v, preferred_element_type=jnp.float32
            )
            return (
                attended.astype(jnp.bfloat16),
                (row_top + jnp.log(row_sum))[:, :, 0],
                jnp.max(row_top[:, :, 0], axis=1),
            )

        return lax.map(attend_block, (row_q, block_ids))

    attended, log_total, block_top = lax.map(
        attend_row, (query_blocks, key_heads, value_heads, row_ids)
    )
    flat_att = attended.reshape(group_rows, head_width)
    branch_a = lax.psum_scatter(
        jnp.dot(flat_att, w_out, preferred_element_type=jnp.float32),
        "tensor",
        scatter_dimension=0,
        tiled=True,
    )
    residual = source + branch_a + out_bias
    normed_b, unit_b, inverse_b = normalize(residual, norm2_gain, norm2_bias)
    whole_b = lax.all_gather(normed_b.astype(jnp.bfloat16), "tensor", axis=0, tiled=True)
    pre_act = jnp.dot(whole_b, w_up, preferred_element_type=jnp.float32) + up_bias
    activated = gelu_tanh(pre_act).astype(jnp.bfloat16)
    branch_b = lax.psum_scatter(
        jnp.dot(activated, w_down, preferred_element_type=jnp.float32).astype(jnp.bfloat16),
        "tensor",
        scatter_dimension=0,
        tiled=True,
    ).astype(jnp.float32)
    hidden_out = (residual + branch_b + down_bias).astype(jnp.bfloat16)
    head_maxima = lax.pmax(jnp.max(block_top, axis=(0, 1)), "dp")
    limit = jnp.float32(CLIP_LIMIT)
    factor = jnp.sqrt(limit / jnp.maximum(head_maxima, limit))
    column = jnp.repeat(factor, HEAD_DIM)
    scaled_qk = (w_qkv[:2].astype(jnp.float32) * column).astype(jnp.bfloat16)
    scaled_query_bias = qv_bias[0] * column
    whole_grad = lax.all_gather(cotangent, "tensor", axis=0, tiled=True)
    grad_act = jnp.einsum("td,fd->tf", whole_grad, w_down, preferred_element_type=jnp.float32)
    grad_pre = jax.vjp(gelu_tanh, pre_act)[1](grad_act)[0].astype(jnp.bfloat16)
    grad_down = jnp.einsum("tf,td->fd", activated, whole_grad, preferred_element_type=jnp.float32)
    grad_up = jnp.einsum("td,tf->df", whole_b, grad_pre, preferred_element_type=jnp.float32)
    grad_up_bias = jnp.sum(grad_pre, axis=0, dtype=jnp.float32)
    grad_norm_b = lax.psum_scatter(
        jnp.einsum("tf,df->td", grad_pre, w_up, preferred_element_type=jnp.float32),
        "tensor",
        scatter_dimension=0,
        tiled=True,
    )
    grad_top = cotangent.astype(jnp.float32)
    grad_resid = grad_top + norm_back(grad_norm_b, unit_b, inverse_b, norm2_gain)
    grad_branch = grad_resid.astype(jnp.bfloat16)
    whole_branch = lax.all_gather(grad_branch, "tensor", axis=0, tiled=True)
    grad_out = jnp.einsum("te,td->ed", flat_att, whole_branch, preferred_element_type=jnp.float32)
    grad_att = jnp.einsum(
        "td,ed->te", whole_branch, w_out, preferred_element_type=jnp.float32
    ).astype(jnp.bfloat16)

    def back_row(parts_in):
        row_q, row_k, row_v, ids_row, row_grad, row_lse = parts_in
        block_ids = ids_row.reshape(block_count, QBLOCK)

        def back_block(state_in, block_in):
            key_grad, value_grad = state_in
            block_q, query_ids, block_grad, block_lse = block_in
            scores = (
                jnp.einsum("qhd,khd->hqk", block_q, row_k, preferred_element_type=jnp.float32)
                * score_scale
            )
            allowed = query_ids[:, None] == ids_row[None, :]
            scores = jnp.where(allowed[None], scores, neg_fill)
            prob_full = jnp.exp(scores - block_lse[:, :, None])
            grad_probs = jnp.einsum(
                "qhd,khd->hqk", block_grad, row_v, preferred_element_type=jnp.float32
            )
            inner = jnp.sum(prob_full * grad_probs, axis=2, keepdims=True)
            grad_scores = (prob_full * (grad_probs - inner)).astype(jnp.bfloat16)
            query_grad = (
                jnp.einsum("hqk,khd->qhd", grad_scores, row_k, preferred_element_type=jnp.float32)
                * score_scale
            )
            key_grad = (
                key_grad
                + jnp.einsum(
                    "hqk,qhd->khd", grad_scores, block_q, preferred_element_type=jnp.float32
                )
                * score_scale
            )
            value_grad = value_grad + jnp.einsum(
                "hqk,qhd->khd",
                prob_full.astype(jnp.bfloat16),
                block_grad,
                preferred_element_type=jnp.float32,
            )
            return ((key_grad, value_grad), query_grad.astype(jnp.bfloat16))

        zero_rows = jnp.zeros(row_k.shape, jnp.float32)
        (key_grad, value_grad), query_grad = lax.scan(
            back_block, (zero_rows, zero_rows), (row_q, block_ids, row_grad, row_lse)
        )
        return (query_grad, key_grad.astype(jnp.bfloat16), value_grad.astype(jnp.bfloat16))

    query_grad, key_grad, value_grad = lax.map(
        back_row,
        (query_blocks, key_heads, value_heads, row_ids, grad_att.reshape(block_shape), log_total),
    )
    grad_stack = jnp.stack(
        [
            query_grad.reshape(group_rows, head_width),
            key_grad.reshape(group_rows, head_width),
            value_grad.reshape(group_rows, head_width),
        ]
    )
    grad_qkv = jnp.einsum("td,cte->cde", whole_a, grad_stack, preferred_element_type=jnp.float32)
    grad_qv_bias = jnp.stack(
        [
            jnp.sum(grad_stack[0], axis=0, dtype=jnp.float32),
            jnp.sum(grad_stack[2], axis=0, dtype=jnp.float32),
        ]
    )
    grad_norm_a = lax.psum_scatter(
        jnp.einsum("cte,cde->td", grad_stack, w_qkv, preferred_element_type=jnp.float32),
        "tensor",
        scatter_dimension=0,
        tiled=True,
    )
    grad_in = (grad_resid + norm_back(grad_norm_a, unit_a, inverse_a, norm1_gain)).astype(
        jnp.bfloat16
    )
    grad_qkv, grad_out, grad_up, grad_down = (
        lax.psum_scatter(grad_qkv, "dp", scatter_dimension=1, tiled=True),
        lax.psum_scatter(grad_out, "dp", scatter_dimension=1, tiled=True),
        lax.psum_scatter(grad_up, "dp", scatter_dimension=0, tiled=True),
        lax.psum_scatter(grad_down, "dp", scatter_dimension=1, tiled=True),
    )
    grad_qv_bias, grad_up_bias = lax.psum((grad_qv_bias, grad_up_bias), "dp")
    shared_part = jnp.stack(
        [
            jnp.sum(grad_norm_a * unit_a, axis=0),
            jnp.sum(grad_norm_a, axis=0),
            jnp.sum(grad_resid, axis=0),
            jnp.sum(grad_norm_b * unit_b, axis=0),
            jnp.sum(grad_norm_b, axis=0),
            jnp.sum(grad_top, axis=0),
        ]
    )
    grad_shared = lax.psum(shared_part, ("dp", "tensor"))
    return (
        hidden_out,
        grad_in,
        grad_qkv,
        grad_out,
        grad_up,
        grad_down,
        grad_qv_bias,
        grad_up_bias,
        grad_shared,
        head_maxima,
        scaled_qk,
        scaled_query_bias,
    )


def solution(mesh):
    return jax.shard_map(
        local,
        mesh=mesh,
        in_specs=(
            P(("dp", "tensor"), None),
            P("dp"),
            P(),
            P(),
            P(None, None, "tensor"),
            P(None, "tensor"),
            P("tensor", None),
            P(),
            P(),
            P(),
            P(None, "tensor"),
            P("tensor"),
            P("tensor", None),
            P(),
            P(("dp", "tensor"), None),
        ),
        out_specs=(
            P(("dp", "tensor"), None),
            P(("dp", "tensor"), None),
            P(None, "dp", "tensor"),
            P("tensor", "dp"),
            P("dp", "tensor"),
            P("tensor", "dp"),
            P(None, "tensor"),
            P("tensor"),
            P(),
            P("tensor"),
            P(None, None, "tensor"),
            P("tensor"),
        ),
        check_vma=False,
    )
```

profile of v0, /device:TPU:0, one launch (start us, length us, event | category | flops | bytes accessed | tf_op | source)
XLA Modules:
  0.0 802.8 jit_solution(1162977882640721757)
XLA Ops:
  7.3 1.4 convert_reduce_fusion.1
  8.6 1.4 fusion.71
  10.0 2.2 fusion.64
  12.5 26.6 %all-gather.5.cloned.1.call-done = bf16[1024,1152]{1,0:T(8,128)(2,1)} async-done(((bf16[256,1152]{1,0:T(8,128)(2,1)}), bf16[1024,1152]{1,0:T(8,128)(2,1)}) %all-gather.5.cloned.1.call-update) | async-done | bytes 2359312 | tf_op jit(solution)/shard_map/all_gather | solution.py:63
  39.2 4.7 fusion.54
  44.0 1.6 fusion.81
  45.6 3.2 squeeze.52
  48.8 2.3 add_convert_fusion.2
  53.0 20.3 %while.51 = (s32[]{:T(128)}, bf16[2,512,4,72]{1,3,2,0:T(8,128)(2,1)}, f32[2,4,512]{2,1,0:T(4,128)S(1)}, f32[2,4]{1,0:T(2,128)S(1)}, s32[2,512]{1,0:T(2,128)S(1)}...) while((s32[]{:T(128)}, ...), condition=%wide.region_6.7_spmd, body=%wide.region_2.6_spmd.sunk | while | flops 631912448 | bytes 36186380 | solution.py:98
  53.4 2.8 fusion.132
  56.2 2.9 fusion.133
  59.2 3.1 fusion.134
  63.6 2.8 fusion.132
  66.4 2.9 fusion.133
  69.3 3.1 fusion.134
  73.4 1.7 copy.37
  76.0 3.6 fusion.82
  80.5 47.2 %reduce-scatter.11.cloned.1.call-done = f32[256,1152]{1,0:T(8,128)} async-done(((f32[1024,1152]{1,0:T(8,128)}), f32[256,1152]{1,0:T(8,128)}) %reduce-scatter.11.cloned.1.call-update) | async-done | bytes 1179664 | tf_op jit(solution)/shard_map/reduce_scatter | solution.py:104
  127.7 1.7 fusion.79
  131.7 21.7 %all-gather.9.cloned.1.call-done = bf16[1024,1152]{1,0:T(8,128)(2,1)} async-done(((bf16[256,1152]{1,0:T(8,128)(2,1)}), bf16[1024,1152]{1,0:T(8,128)(2,1)}) %all-gather.9.cloned.1.call-update) | async-done | bytes 2359312 | tf_op jit(solution)/shard_map/all_gather | solution.py:128
  153.5 7.5 fusion.83
  161.0 18.6 %all-gather.7.cloned.1.call-done = bf16[1024,1152]{1,0:T(8,128)(2,1)} async-done(((bf16[256,1152]{1,0:T(8,128)(2,1)}), bf16[1024,1152]{1,0:T(8,128)(2,1)}) %all-gather.7.cloned.1.call-update) | async-done | bytes 2359312 | tf_op jit(solution)/shard_map/all_gather | solution.py:112
  179.6 9.9 %convert_reduce_fusion = (f32[1076]{0:T(1024)}, bf16[1024,1076]{0,1:T(8,128)(2,1)S(1)}, f32[1024,1076]{0,1:T(8,128)}) fusion(f32[1024,1076]{0,1:T(8,128)} %fusion.83, f32[1076]{0:T(1024)S(1)} %copy-done.48, bf16[1024,1152]{1,0:T(8,128)(2,1)} %all-gather.7.cloned.1.call-done, bf16[1152,1076]{0,1:T(8,128)(2,1)S(1)} %copy-done), kind=kOutput, calls=%fused_computation.63 | convolution fusion | flops 2563943424 | bytes 15865248 | tf_op jit(solution)/shard_map/dot_general | solution.py:113
  189.5 1.4 copy-done.50
  190.9 5.2 fusion.84
  196.2 1.6 copy-done.47
  197.8 7.5 convolution_convert_fusion
  205.4 38.8 %reduce-scatter.15.cloned.1.call-done = f32[256,1152]{1,0:T(8,128)} async-done(((f32[1024,1152]{1,0:T(8,128)}), f32[256,1152]{1,0:T(8,128)}) %reduce-scatter.15.cloned.1.call-update) | async-done | bytes 1179664 | tf_op jit(solution)/shard_map/reduce_scatter | solution.py:134
  244.1 2.4 multiply_reduce_fusion.1
  246.5 33.1 %reduce-scatter.13.cloned.1.call-done = bf16[256,1152]{1,0:T(8,128)(2,1)} async-done(((bf16[1024,1152]{1,0:T(8,128)(2,1)}), bf16[256,1152]{1,0:T(8,128)(2,1)}) %reduce-scatter.13.cloned.1.call-update) | async-done | bytes 589840 | tf_op jit(solution)/shard_map/reduce_scatter | solution.py:115
  279.6 3.6 fusion.77
  284.5 23.9 %all-gather.11.cloned.1.call-done = bf16[1024,1152]{1,0:T(8,128)(2,1)} async-done(((bf16[256,1152]{1,0:T(8,128)(2,1)}), bf16[1024,1152]{1,0:T(8,128)(2,1)}) %all-gather.11.cloned.1.call-update) | async-done | bytes 2359312 | tf_op jit(solution)/shard_map/all_gather | solution.py:143
  308.4 3.6 convolution_convert_fusion.1
  312.0 2.3 squeeze.54
  316.0 25.9 %while.52 = (s32[]{:T(128)}, f32[1024,4,72]{0,2,1:T(8,128)S(1)}, f32[1024,4,72]{0,2,1:T(8,128)}, bf16[2,512,4,72]{1,3,2,0:T(8,128)(2,1)}, bf16[2,512,4,72]{1,3,2...) while((s32[]{:T(128)}, f32[1024,4,72]{0,2,1:T(8,128)S(1)}, ...), condition=%wide.region_16.17_spmd.clone, body=%wide.region_14.16_spmd.clone.sunk | while | flops 1543698432 | bytes 91916632 | solution.py:188
  317.8 2.6 fusion.146
  320.5 3.3 multiply_reduce_fusion.7
  323.8 2.4 multiply_convert_fusion.6
  326.3 1.4 fusion.147
  330.6 2.6 fusion.146
  333.3 3.3 multiply_reduce_fusion.7
  336.6 2.4 multiply_convert_fusion.6
  339.0 1.4 fusion.147
  342.0 1.9 copy.39
  344.6 6.3 convolution_bitcast_fusion.1
  350.9 8.6 %copy.41 = f32[3,1152,288]{2,0,1:T(4,128)} copy(f32[3,1152,288]{1,2,0:T(8,128)} %convolution_bitcast_fusion.1) | data formatting | bytes 7962624
  359.5 9.0 %reshape.211 = f32[1152,864]{1,0:T(8,128)} reshape(f32[1152,3,288]{2,1,0:T(4,128)} %bitcast.143) | data formatting | bytes 7962624
  368.5 1.5 copy-done.21
  370.1 6.3 convolution_bitcast_fusion
  376.5 8.6 %fusion.76 = f32[1076,1152]{0,1:T(8,128)} fusion(bf16[1024,1152]{1,0:T(8,128)(2,1)} %all-gather.9.cloned.1.call-done, f32[1024,1076]{0,1:T(8,128)} %get-tuple-element.355), kind=kOutput, calls=%fused_computation.124 | convolution fusion | flops 2548518912 | bytes 11724800 | tf_op jit(solution)/shard_map/tf,td->fd/dot_general | solution.py:131
  385.4 8.0 fusion.86
  394.5 4.4 fusion.85
  399.1 22.0 %pmax.7 = f32[4]{0:T(128)S(1)} all-reduce(f32[4]{0:T(128)S(1)} %reduce_max.27), channel_id=1, replica_groups=mesh['dp'=8,'tensor'=4] {'dp'}, use_global_device_ids=true, to_apply=%region_37.38 | all-reduce | flops 4 | bytes 32 | tf_op jit(solution)/shard_map/pmax | solution.py:122
  421.8 1.3 multiply_convert_fusion.2
  423.7 34.2 %all-reduce = (f32[2,288]{1,0:T(2,128)}, f32[1076]{0:T(1024)}) all-reduce(f32[2,288]{1,0:T(2,128)S(1)} %pad_maximum_fusion.3, f32[1076]{0:T(1024)S(1)} %copy-done.43), channel_id=1, replica_groups=mesh['dp'=8,'tensor'=4] {'dp'}, use_global_device_ids=true, to_apply=%region_26.27 | all-reduce | flops 1652 | bytes 13216 | tf_op jit(solution)/shard_map/psum | solution.py:226
  457.9 2.4 reshape.212
  460.3 2.2 copy.40
  462.5 44.9 %reduce-scatter.17.cloned.1.call-done = f32[256,1152]{1,0:T(8,128)} async-done(((f32[1024,1152]{1,0:T(8,128)}), f32[256,1152]{1,0:T(8,128)}) %reduce-scatter.17.cloned.1.call-update) | async-done | bytes 1179664 | tf_op jit(solution)/shard_map/reduce_scatter | solution.py:211
  507.4 1.9 fusion.70
  509.3 42.9 %psum.23 = f32[6,1152]{1,0:T(8,128)} all-reduce(f32[6,1152]{1,0:T(8,128)S(1)} %stack.43), channel_id=1, replica_groups=mesh['dp'=8,'tensor'=4] {'dp','tensor'}, use_global_device_ids=true, to_apply=%region_35.36 | all-reduce | flops 6912 | bytes 55296 | tf_op jit(solution)/shard_map/psum | solution.py:237
  552.2 2.9 fusion.69
  555.1 62.2 %reduce-scatter.23.cloned.1.call-done = f32[1076,144]{0,1:T(8,128)} async-done(((f32[1076,1152]{0,1:T(8,128)}), f32[1076,144]{0,1:T(8,128)}) %reduce-scatter.23.cloned.1.call-update) | async-done | bytes 619792 | tf_op jit(solution)/shard_map/reduce_scatter | solution.py:224
  617.3 108.1 %reduce-scatter.21.cloned.1.call-done = f32[144,1076]{1,0:T(8,128)} async-done(((f32[1152,1076]{1,0:T(8,128)}), f32[144,1076]{1,0:T(8,128)}) %reduce-scatter.21.cloned.1.call-update) | async-done | bytes 619792 | tf_op jit(solution)/shard_map/reduce_scatter | solution.py:223
  725.4 70.3 %reduce-scatter.19.cloned.1.call-done = f32[288,144]{0,1:T(8,128)} async-done(((f32[288,1152]{0,1:T(8,128)}), f32[288,144]{0,1:T(8,128)}) %reduce-scatter.19.cloned.1.call-update) | async-done | bytes 165904 | tf_op jit(solution)/shard_map/reduce_scatter | solution.py:222
  (203 shorter events, 21.1 us)
Async XLA Ops:
  7.2 172.5 %copy-start = (bf16[1152,1076]{0,1:T(8,128)(2,1)S(1)}, bf16[1152,1076]{0,1:T(8,128)(2,1)}, u32[]{:S(2)}) copy-start(bf16[1152,1076]{0,1:T(8,128)(2,1)} %param.29) | copy-start | bytes 7437316
  7.2 5.1 copy-start.27
  7.2 5.1 copy-start.44
  7.2 32.0 %all-gather.5.cloned.1.call-start = ((), (), s32[]{:S(2)}) async-start(), calls=%async_computation.8 | async-start | bytes 2949120 | tf_op jit(solution)/shard_map/all_gather | solution.py:63
  8.6 30.5 %copy-start.34 = (f32[256]{0:T(256)}, f32[256]{0:T(256)S(1)}, u32[]{:S(2)}) copy-start(f32[256]{0:T(256)S(1)} %broadcast_multiply_fusion.5) | copy-start | bytes 3076
  10.0 29.2 %copy-start.38 = (f32[256]{0:T(256)}, f32[256]{0:T(256)S(1)}, u32[]{:S(2)}) copy-start(f32[256]{0:T(256)S(1)} %add_rsqrt_fusion.1) | copy-start | bytes 3076
  12.2 115.5 %reduce-scatter.11.cloned.1.call-start = ((), (), s32[]{:S(2)}) async-start(), calls=%async_computation.9 | async-start | bytes 5898240 | tf_op jit(solution)/shard_map/reduce_scatter | solution.py:104
  12.4 31.6 %copy-start.36 = (f32[288]{0:T(512)}, f32[288]{0:T(512)S(1)}, u32[]{:S(2)}) copy-start(f32[288]{0:T(512)S(1)} %get-tuple-element.296) | copy-start | bytes 3460
  48.8 2.3 copy-start.13
  56.2 2.9 copy-start.5
  56.2 2.9 copy-start.16
  66.4 2.9 copy-start.5
  66.4 2.9 copy-start.16
  73.3 6.3 copy-start.45
  73.4 2.7 copy-start.22
  79.7 48.0 %copy-start.40 = (f32[1152]{0:T(1024)S(1)}, f32[1152]{0:T(1024)}, u32[]{:S(2)}) copy-start(f32[1152]{0:T(1024)} %param.26) | copy-start | bytes 13828
  79.7 50.7 %copy-start.28 = (f32[1152]{0:T(1024)S(1)}, f32[1152]{0:T(1024)}, u32[]{:S(2)}) copy-start(f32[1152]{0:T(1024)} %param.27) | copy-start | bytes 13828
  79.7 50.7 %copy-start.41 = (f32[1152]{0:T(1024)S(1)}, f32[1152]{0:T(1024)}, u32[]{:S(2)}) copy-start(f32[1152]{0:T(1024)} %param.28) | copy-start | bytes 13828
  79.7 73.7 %all-gather.9.cloned.1.call-start = ((), (), s32[]{:S(2)}) async-start(), calls=%async_computation.12 | async-start | bytes 2949120 | tf_op jit(solution)/shard_map/all_gather | solution.py:128
  80.5 99.2 %all-gather.7.cloned.1.call-start = ((), (), s32[]{:S(2)}) async-start(), calls=%async_computation.10 | async-start | bytes 2949120 | tf_op jit(solution)/shard_map/all_gather | solution.py:112
  131.5 48.1 %copy-start.48 = (f32[1076]{0:T(1024)S(1)}, f32[1076]{0:T(1024)}, u32[]{:S(2)}) copy-start(f32[1076]{0:T(1024)} %param.30) | copy-start | bytes 12916
  131.5 112.6 %reduce-scatter.15.cloned.1.call-start = ((), (), s32[]{:S(2)}) async-start(), calls=%async_computation.13 | async-start | bytes 5898240 | tf_op jit(solution)/shard_map/reduce_scatter | solution.py:134
  189.5 1.4 copy-start.50
  196.1 1.7 copy-start.47
  196.1 83.5 %reduce-scatter.13.cloned.1.call-start = ((), (), s32[]{:S(2)}) async-start(), calls=%async_computation.11 | async-start | bytes 2949120 | tf_op jit(solution)/shard_map/reduce_scatter | solution.py:115
  205.3 38.8 %copy-start.4 = (f32[256,1152]{1,0:T(8,128)S(1)}, f32[256,1152]{1,0:T(8,128)}, u32[]{:S(2)}) copy-start(f32[256,1152]{1,0:T(8,128)} %copy-done.3) | copy-start | bytes 3538948
  205.3 74.3 %copy-start.42 = (f32[1152]{0:T(1024)S(1)}, f32[1152]{0:T(1024)}, u32[]{:S(2)}) copy-start(f32[1152]{0:T(1024)} %param.32) | copy-start | bytes 13828
  205.3 103.1 %all-gather.11.cloned.1.call-start = ((), (), s32[]{:S(2)}) async-start(), calls=%async_computation.14 | async-start | bytes 2949120 | tf_op jit(solution)/shard_map/all_gather | solution.py:143
  283.2 25.2 %copy-start.8 = (f32[256,1152]{1,0:T(8,128)}, f32[256,1152]{1,0:T(8,128)S(1)}, u32[]{:S(2)}) copy-start(f32[256,1152]{1,0:T(8,128)S(1)} %get-tuple-element.340) | copy-start | bytes 3538948
  284.2 173.7 %reduce-scatter.25.cloned.1.call-start = ((), (), s32[]{:S(2)}) async-start(), calls=%async_computation.19 | async-start | bytes 4644864
  312.0 4.0 copy-start.2
  316.4 1.3 copy-start.9
  316.4 1.4 copy-start.18
  317.8 2.7 copy-start.6
  320.5 3.3 copy-start.19
  323.8 2.4 copy-start.10
  329.2 1.4 copy-start.18
  330.6 2.7 copy-start.6
  333.3 3.3 copy-start.19
  336.6 2.4 copy-start.10
  341.9 2.5 copy-start.20
  342.0 8.9 %copy-start.23 = (bf16[1024,4,72]{0,2,1:T(8,128)(2,1)}, bf16[1024,4,72]{0,2,1:T(8,128)(2,1)S(1)}, u32[]{:S(2)}) copy-start(bf16[1024,4,72]{0,2,1:T(8,128)(2,1)S(1)} %convert_element_type.109) | copy-start | bytes 1769476
  344.4 6.5 copy-start.25
  344.6 6.4 copy-start.26
  368.5 1.6 copy-start.21
  368.5 1.7 copy-start.24
  368.5 138.9 %reduce-scatter.17.cloned.1.call-start = ((), (), s32[]{:S(2)}) async-start(), calls=%async_computation.15 | async-start | bytes 5898240 | tf_op jit(solution)/shard_map/reduce_scatter | solution.py:211
  376.5 240.9 %reduce-scatter.23.cloned.1.call-start = ((), (), s32[]{:S(2)}) async-start(), calls=%async_computation.18 | async-start | bytes 5971968 | tf_op jit(solution)/shard_map/reduce_scatter | solution.py:224
  385.2 340.2 %reduce-scatter.21.cloned.1.call-start = ((), (), s32[]{:S(2)}) async-start(), calls=%async_computation.17 | async-start | bytes 5971968 | tf_op jit(solution)/shard_map/reduce_scatter | solution.py:223
  393.4 5.6 copy-start.46
  393.5 27.8 %copy-start.37 = (f32[288]{0:T(512)S(1)}, f32[288]{0:T(512)}, u32[]{:S(2)}) copy-start(f32[288]{0:T(512)} %copy-done.36) | copy-start | bytes 3460
  393.5 402.3 %reduce-scatter.19.cloned.1.call-start = ((), (), s32[]{:S(2)}) async-start(), calls=%async_computation.16 | async-start | bytes 1990656 | tf_op jit(solution)/shard_map/reduce_scatter | solution.py:222
  399.0 24.2 %copy-start.31 = (f32[1152]{0:T(1024)S(1)}, f32[1152]{0:T(1024)}, u32[]{:S(2)}) copy-start(f32[1152]{0:T(1024)} %get-tuple-element.287) | copy-start | bytes 13828
  399.0 24.2 %copy-start.33 = (f32[1152]{0:T(1024)S(1)}, f32[1152]{0:T(1024)}, u32[]{:S(2)}) copy-start(f32[1152]{0:T(1024)} %get-tuple-element.339) | copy-start | bytes 13828
  399.0 24.2 %copy-start.32 = (f32[1152]{0:T(1024)S(1)}, f32[1152]{0:T(1024)}, u32[]{:S(2)}) copy-start(f32[1152]{0:T(1024)} %get-tuple-element.354) | copy-start | bytes 13828
  399.0 24.3 %copy-start.30 = (f32[1152]{0:T(1024)S(1)}, f32[1152]{0:T(1024)}, u32[]{:S(2)}) copy-start(f32[1152]{0:T(1024)} %get-tuple-element.293) | copy-start | bytes 13828
  399.0 24.3 %copy-start.12 = (bf16[2,512,4,72]{1,3,2,0:T(8,128)(2,1)S(1)}, bf16[2,512,4,72]{1,3,2,0:T(8,128)(2,1)}, u32[]{:S(2)}) copy-start(bf16[2,512,4,72]{1,3,2,0:T(8,128)(2,1)} %get-tuple-element.176) | copy-start | bytes 1769476
  399.0 24.6 %copy-start.43 = (f32[1076]{0:T(1024)S(1)}, f32[1076]{0:T(1024)}, u32[]{:S(2)}) copy-start(f32[1076]{0:T(1024)} %get-tuple-element.341) | copy-start | bytes 12916
  421.1 39.2 %copy-start.49 = (f32[4]{0:T(128)}, f32[4]{0:T(128)S(1)}, u32[]{:S(2)}) copy-start(f32[4]{0:T(128)S(1)} %pmax.7) | copy-start | bytes 52
  423.2 84.2 %copy-start.7 = (bf16[256,1152]{1,0:T(8,128)(2,1)S(1)}, bf16[256,1152]{1,0:T(8,128)(2,1)}, u32[]{:S(2)}) copy-start(bf16[256,1152]{1,0:T(8,128)(2,1)} %param.19) | copy-start | bytes 1769476
  423.2 84.2 %copy-start.29 = (f32[1152]{0:T(1024)S(1)}, f32[1152]{0:T(1024)}, u32[]{:S(2)}) copy-start(f32[1152]{0:T(1024)} %param.21) | copy-start | bytes 13828
  423.2 84.2 %copy-start.35 = (f32[256]{0:T(256)S(1)}, f32[256]{0:T(256)}, u32[]{:S(2)}) copy-start(f32[256]{0:T(256)} %copy-done.34) | copy-start | bytes 3076
  423.2 84.2 %copy-start.39 = (f32[256]{0:T(256)S(1)}, f32[256]{0:T(256)}, u32[]{:S(2)}) copy-start(f32[256]{0:T(256)} %copy-done.38) | copy-start | bytes 3076
  460.3 335.5 %copy-start.1 = (bf16[1152,1076]{0,1:T(8,128)(2,1)S(1)}, bf16[1152,1076]{0,1:T(8,128)(2,1)}, u32[]{:S(2)}) copy-start(bf16[1152,1076]{0,1:T(8,128)(2,1)} %param.29) | copy-start | bytes 7437316
  (8 other events, 8.0 us)
Sparse Core Ops, SparseCore 0:
  12.4 26.7 all-gather.4
  79.8 47.8 reduce-scatter.10
  129.4 24.0 all-gather.8
  155.5 24.0 all-gather.6
  196.2 47.8 reduce-scatter.14
  246.5 33.0 reduce-scatter.12
  284.3 24.0 all-gather.10
  368.6 88.3 reduce-scatter.24
  459.6 47.7 reduce-scatter.16
  511.8 105.4 reduce-scatter.22
  621.5 103.8 reduce-scatter.20
  729.7 65.9 reduce-scatter.18
where the time goes:
time: 812 us; the launch traced here: 803 us
  waiting for transfers between devices  496 us (61%)
  matrix products  107 us (13%)
  blocking collectives  99.1 us (12%)
  local copies, waits for them, and re-layouts  46 us (6%)
  other arithmetic  37.6 us (5%)
  between operations  14.9 us (2%)
    reduce_scatter x1, waiting for transfers between devices, local(): lax.psum_scatter(grad_up, 'dp', scatter_dimension=0, tiled=True)  108 us
    reduce_scatter x1, waiting for transfers between devices, local(): lax.psum_scatter(grad_out, 'dp', scatter_dimension=1, tiled=True)  70.3 us
    reduce_scatter x1, waiting for transfers between devices, local(): lax.psum_scatter(grad_down, 'dp', scatter_dimension=1, tiled=True)  62.2 us
    reduce_scatter x1, waiting for transfers between devices, local(): lax.psum_scatter(jnp.dot(flat_att, w_out, preferred_element_type=jnp.floa...  47.2 us
    reduce_scatter x1, waiting for transfers between devices, local(): lax.psum_scatter(jnp.einsum('cte,cde->td', grad_stack, w_qkv, preferred_e...  44.9 us
    psum x1, blocking collectives, local(): grad_shared = lax.psum(shared_part, ('dp', 'tensor'))  42.9 us
    reduce_scatter x1, waiting for transfers between devices, local(): lax.psum_scatter(jnp.einsum('tf,df->td', grad_pre, w_up, preferred_elemen...  38.8 us
    psum x1, blocking collectives, local(): grad_qv_bias, grad_up_bias = lax.psum((grad_qv_bias, grad_up_bias), 'dp')  34.2 us
  transfers between devices with their start and end apart: 12, of which 11 were waited for; matrix products, arithmetic and copies ran while one was open for 7% of the time, Pallas kernels for 0%

commit v1 on v0

--- a/solution.py
+++ b/solution.py
@@ -125,7 +125,14 @@
     column = jnp.repeat(factor, HEAD_DIM)
     scaled_qk = (w_qkv[:2].astype(jnp.float32) * column).astype(jnp.bfloat16)
     scaled_query_bias = qv_bias[0] * column
-    whole_grad = lax.all_gather(cotangent, "tensor", axis=0, tiled=True)
+    ring = [cotangent]
+    for hop in range(3):
+        ring.append(lax.ppermute(ring[-1], "tensor", [(dev, (dev + 1) % 4) for dev in range(4)]))
+    whole_grad = jnp.roll(
+        jnp.concatenate(ring[::-1], axis=0),
+        (lax.axis_index("tensor") + 1) * ring[0].shape[0],
+        axis=0,
+    )
     grad_act = jnp.einsum("td,fd->tf", whole_grad, w_down, preferred_element_type=jnp.float32)
     grad_pre = jax.vjp(gelu_tanh, pre_act)[1](grad_act)[0].astype(jnp.bfloat16)
     grad_down = jnp.einsum("tf,td->fd", activated, whole_grad, preferred_element_type=jnp.float32)

time: 812 us -> 812 us (level)
  local copies, waits for them, and re-layouts: 46 us -> 57.8 us
  waiting for transfers between devices: 496 us -> 485 us
    ppermute x0 -> x3, waiting for transfers between devices: none -> 28.8 us  [local(): lax.ppermute(ring[-1], 'tensor', [(dev, (dev + 1) % 4) for dev in range(4)])]
    all_gather x1 -> x0, waiting for transfers between devices: 21.7 us -> none  [local(): whole_grad = lax.all_gather(cotangent, 'tensor', axis=0, tiled=True)]
    all_gather x1, waiting for transfers between devices: 18.6 us -> 0.01 us  [local(): lax.all_gather(normed_b.astype(jnp.bfloat16), 'tensor', axis=0, tiled=True)]
    unnamed x90 -> x101, local copies, waits for them, and re-layouts: 30.4 us -> 41.4 us
  transfers between devices with their start and end apart: 12 -> 14, of which waited for: 11 -> 11; matrix products, arithmetic and copies ran while one was open for 7% -> 8% of each run, Pallas kernels for 0% -> 0%
where the time goes in v1:
time: 812 us; the launch traced here: 802 us
  waiting for transfers between devices  485 us (60%)
  matrix products  105 us (13%)
  blocking collectives  99.2 us (12%)
  local copies, waits for them, and re-layouts  57.8 us (7%)
  other arithmetic  37.6 us (5%)
  between operations  14.6 us (2%)
    reduce_scatter x1, waiting for transfers between devices, local(): lax.psum_scatter(grad_up, 'dp', scatter_dimension=0, tiled=True)  108 us
    reduce_scatter x1, waiting for transfers between devices, local(): lax.psum_scatter(grad_out, 'dp', scatter_dimension=1, tiled=True)  70.1 us
    reduce_scatter x1, waiting for transfers between devices, local(): lax.psum_scatter(grad_down, 'dp', scatter_dimension=1, tiled=True)  62 us
    reduce_scatter x1, waiting for transfers between devices, local(): lax.psum_scatter(jnp.dot(flat_att, w_out, preferred_element_type=jnp.floa...  47.6 us
    reduce_scatter x1, waiting for transfers between devices, local(): lax.psum_scatter(jnp.einsum('cte,cde->td', grad_stack, w_qkv, preferred_e...  44.7 us
    psum x1, blocking collectives, local(): grad_shared = lax.psum(shared_part, ('dp', 'tensor'))  43 us
    unnamed x101, local copies, waits for them, and re-layouts  41.4 us
    reduce_scatter x1, waiting for transfers between devices, local(): lax.psum_scatter(jnp.einsum('tf,df->td', grad_pre, w_up, preferred_elemen...  40.4 us
  transfers between devices with their start and end apart: 14, of which 11 were waited for; matrix products, arithmetic and copies ran while one was open for 8% of the time, Pallas kernels for 0%

profile of v1, /device:TPU:0, one launch (start us, length us, event | category | flops | bytes accessed | tf_op | source)
XLA Modules:
  0.0 802.3 jit_solution(16639380123264990548)
XLA Ops:
  10.0 2.2 fusion.70
  12.5 26.6 %all-gather.4.cloned.1.call-done = bf16[1024,1152]{1,0:T(8,128)(2,1)} async-done(((bf16[256,1152]{1,0:T(8,128)(2,1)}), bf16[1024,1152]{1,0:T(8,128)(2,1)}) %all-gather.4.cloned.1.call-update) | async-done | bytes 2359312 | tf_op jit(solution)/shard_map/all_gather | solution.py:63
  39.2 4.7 fusion.60
  44.0 1.6 fusion.87
  45.6 3.2 squeeze.52
  48.8 2.3 add_convert_fusion.2
  53.0 20.3 %while.51 = (s32[]{:T(128)}, bf16[2,512,4,72]{1,3,2,0:T(8,128)(2,1)}, f32[2,4,512]{2,1,0:T(4,128)S(1)}, f32[2,4]{1,0:T(2,128)S(1)}, s32[2,512]{1,0:T(2,128)S(1)}...) while((s32[]{:T(128)}, ...), condition=%wide.region_6.7_spmd, body=%wide.region_2.6_spmd.sunk | while | flops 631912448 | bytes 36186380 | solution.py:98
  53.4 2.8 fusion.135
  56.2 2.9 fusion.136
  59.2 3.1 fusion.137
  63.6 2.8 fusion.135
  66.4 2.9 fusion.136
  69.3 3.1 fusion.137
  73.4 1.7 copy.37
  76.0 3.7 fusion.88
  80.1 47.6 %reduce-scatter.11.cloned.1.call-done = f32[256,1152]{1,0:T(8,128)} async-done(((f32[1024,1152]{1,0:T(8,128)}), f32[256,1152]{1,0:T(8,128)}) %reduce-scatter.11.cloned.1.call-update) | async-done | bytes 1179664 | tf_op jit(solution)/shard_map/reduce_scatter | solution.py:104
  127.8 1.7 fusion.85
  131.7 9.6 %collective-permute-done.1 = bf16[256,1152]{1,0:T(8,128)(2,1)} collective-permute-done((bf16[256,1152]{1,0:T(8,128)(2,1)}, bf16[256,1152]{1,0:T(8,128)(2,1)}, u32[]{:S(2)}, u32[]{:S(2)}) %collective-permute-start.1) | collective-permute-done | bytes 589856 | tf_op jit(solution)/shard_map/ppermute | solution.py:130
  141.5 19.2 %collective-permute-done.2 = bf16[256,1152]{1,0:T(8,128)(2,1)} collective-permute-done((bf16[256,1152]{1,0:T(8,128)(2,1)}, bf16[256,1152]{1,0:T(8,128)(2,1)}, u32[]{:S(2)}, u32[]{:S(2)}) %collective-permute-start.2) | collective-permute-done | bytes 589856 | tf_op jit(solution)/shard_map/ppermute | solution.py:130
  160.7 2.0 constant_dynamic-update-slice_fusion.7
  162.6 1.9 constant_dynamic-update-slice_fusion.6
  164.5 1.9 constant_dynamic-update-slice_fusion.5
  167.3 1.9 constant_dynamic-update-slice_fusion.3
  169.3 2.0 constant_dynamic-update-slice_fusion.2
  171.3 2.0 constant_dynamic-update-slice_fusion.1
  174.1 5.5 convolution_add_fusion
  179.6 10.1 %convert_reduce_fusion = (f32[1076]{0:T(1024)}, bf16[1024,1076]{0,1:T(8,128)(2,1)S(1)}) fusion(f32[1024,1076]{0,1:T(8,128)S(1)} %convolution_add_fusion, bf16[1076,1152]{1,0:T(8,128)(2,1)S(1)} %copy-done, bf16[2048,1152]{1,0:T(8,128)(2,1)} %constant_dynamic-update-slice_fusion, s32[]{:T(128)S(6)} %select_n.21), kind=kOutput, calls=%fused_computation.63 | convolution fusion | flops 2562841600 | bytes 11453652 | tf_op jit(solution)/shard_map/td,fd->tf/dot_general | solution.py:136
  189.7 1.4 copy-done.52
  191.2 5.2 fusion.89
  196.5 7.5 convolution_convert_fusion
  204.1 40.4 %reduce-scatter.15.cloned.1.call-done = f32[256,1152]{1,0:T(8,128)} async-done(((f32[1024,1152]{1,0:T(8,128)}), f32[256,1152]{1,0:T(8,128)}) %reduce-scatter.15.cloned.1.call-update) | async-done | bytes 1179664 | tf_op jit(solution)/shard_map/reduce_scatter | solution.py:141
  244.5 2.4 multiply_reduce_fusion.1
  246.8 33.1 %reduce-scatter.13.cloned.1.call-done = bf16[256,1152]{1,0:T(8,128)(2,1)} async-done(((bf16[1024,1152]{1,0:T(8,128)(2,1)}), bf16[256,1152]{1,0:T(8,128)(2,1)}) %reduce-scatter.13.cloned.1.call-update) | async-done | bytes 589840 | tf_op jit(solution)/shard_map/reduce_scatter | solution.py:115
  280.0 3.6 fusion.84
  284.8 23.9 %all-gather.8.cloned.1.call-done = bf16[1024,1152]{1,0:T(8,128)(2,1)} async-done(((bf16[256,1152]{1,0:T(8,128)(2,1)}), bf16[1024,1152]{1,0:T(8,128)(2,1)}) %all-gather.8.cloned.1.call-update) | async-done | bytes 2359312 | tf_op jit(solution)/shard_map/all_gather | solution.py:150
  308.8 3.6 convolution_convert_fusion.1
  312.4 2.3 squeeze.54
  316.4 25.9 %while.52 = (s32[]{:T(128)}, f32[1024,4,72]{0,2,1:T(8,128)S(1)}, f32[1024,4,72]{0,2,1:T(8,128)}, bf16[2,512,4,72]{1,3,2,0:T(8,128)(2,1)}, bf16[2,512,4,72]{1,3,2...) while((s32[]{:T(128)}, f32[1024,4,72]{0,2,1:T(8,128)S(1)}, ...), condition=%wide.region_16.17_spmd.clone, body=%wide.region_14.16_spmd.clone.sunk | while | flops 1543698432 | bytes 91916632 | solution.py:195
  318.2 2.6 fusion.149
  320.9 3.3 multiply_reduce_fusion.7
  324.2 2.4 multiply_convert_fusion.6
  331.0 2.6 fusion.149
  333.7 3.3 multiply_reduce_fusion.7
  337.0 2.4 multiply_convert_fusion.6
  342.4 1.9 copy.39
  344.9 6.3 convolution_bitcast_fusion.1
  351.2 8.6 %copy.41 = f32[3,1152,288]{2,0,1:T(4,128)} copy(f32[3,1152,288]{1,2,0:T(8,128)} %convolution_bitcast_fusion.1) | data formatting | bytes 7962624
  359.8 8.9 %reshape.211 = f32[1152,864]{1,0:T(8,128)} reshape(f32[1152,3,288]{2,1,0:T(4,128)} %bitcast.141) | data formatting | bytes 7962624
  368.8 1.5 copy-done.22
  370.4 6.3 convolution_bitcast_fusion
  376.8 8.7 %fusion.54 = f32[1076,1152]{0,1:T(8,128)} fusion(bf16[2048,1152]{1,0:T(8,128)(2,1)} %constant_dynamic-update-slice_fusion, s32[]{:T(128)S(6)} %select_n.21, f32[1024,1076]{0,1:T(8,128)} %copy-done.51), kind=kOutput, calls=%fused_computation.72 | convolution fusion | flops 2548518912 | bytes 11741188 | tf_op jit(solution)/shard_map/tf,td->fd/dot_general | solution.py:138
  385.8 8.0 fusion.91
  394.9 4.5 fusion.90
  399.4 22.0 %pmax.7 = f32[4]{0:T(128)S(1)} all-reduce(f32[4]{0:T(128)S(1)} %reduce_max.27), channel_id=1, replica_groups=mesh['dp'=8,'tensor'=4] {'dp'}, use_global_device_ids=true, to_apply=%region_37.38 | all-reduce | flops 4 | bytes 32 | tf_op jit(solution)/shard_map/pmax | solution.py:122
  424.1 34.2 %all-reduce = (f32[2,288]{1,0:T(2,128)}, f32[1076]{0:T(1024)}) all-reduce(f32[2,288]{1,0:T(2,128)S(1)} %pad_maximum_fusion.3, f32[1076]{0:T(1024)S(1)} %copy-done.44), channel_id=1, replica_groups=mesh['dp'=8,'tensor'=4] {'dp'}, use_global_device_ids=true, to_apply=%region_26.27 | all-reduce | flops 1652 | bytes 13216 | tf_op jit(solution)/shard_map/psum | solution.py:233
  458.3 2.4 reshape.212
  460.7 2.2 copy.40
  462.9 44.7 %reduce-scatter.17.cloned.1.call-done = f32[256,1152]{1,0:T(8,128)} async-done(((f32[1024,1152]{1,0:T(8,128)}), f32[256,1152]{1,0:T(8,128)}) %reduce-scatter.17.cloned.1.call-update) | async-done | bytes 1179664 | tf_op jit(solution)/shard_map/reduce_scatter | solution.py:218
  507.6 1.9 fusion.76
  509.6 43.0 %psum.23 = f32[6,1152]{1,0:T(8,128)} all-reduce(f32[6,1152]{1,0:T(8,128)S(1)} %stack.43), channel_id=1, replica_groups=mesh['dp'=8,'tensor'=4] {'dp','tensor'}, use_global_device_ids=true, to_apply=%region_35.36 | all-reduce | flops 6912 | bytes 55296 | tf_op jit(solution)/shard_map/psum | solution.py:244
  552.5 2.9 fusion.75
  555.5 62.0 %reduce-scatter.23.cloned.1.call-done = f32[1076,144]{0,1:T(8,128)} async-done(((f32[1076,1152]{0,1:T(8,128)}), f32[1076,144]{0,1:T(8,128)}) %reduce-scatter.23.cloned.1.call-update) | async-done | bytes 619792 | tf_op jit(solution)/shard_map/reduce_scatter | solution.py:231
  617.5 108.0 %reduce-scatter.21.cloned.1.call-done = f32[144,1076]{1,0:T(8,128)} async-done(((f32[1152,1076]{1,0:T(8,128)}), f32[144,1076]{1,0:T(8,128)}) %reduce-scatter.21.cloned.1.call-update) | async-done | bytes 619792 | tf_op jit(solution)/shard_map/reduce_scatter | solution.py:230
  725.4 70.1 %reduce-scatter.19.cloned.1.call-done = f32[288,144]{0,1:T(8,128)} async-done(((f32[288,1152]{0,1:T(8,128)}), f32[288,144]{0,1:T(8,128)}) %reduce-scatter.19.cloned.1.call-update) | async-done | bytes 165904 | tf_op jit(solution)/shard_map/reduce_scatter | solution.py:229
  (218 shorter events, 29.4 us)
Async XLA Ops:
  7.2 172.4 %copy-start = (bf16[1076,1152]{1,0:T(8,128)(2,1)S(1)}, bf16[1076,1152]{1,0:T(8,128)(2,1)}, u32[]{:S(2)}) copy-start(bf16[1076,1152]{1,0:T(8,128)(2,1)} %param.31) | copy-start | bytes 7437316
  7.2 5.1 copy-start.28
  7.2 5.1 copy-start.45
  7.2 32.0 %all-gather.4.cloned.1.call-start = ((), (), s32[]{:S(2)}) async-start(), calls=%async_computation.8 | async-start | bytes 2949120 | tf_op jit(solution)/shard_map/all_gather | solution.py:63
  8.6 30.5 %copy-start.35 = (f32[256]{0:T(256)}, f32[256]{0:T(256)S(1)}, u32[]{:S(2)}) copy-start(f32[256]{0:T(256)S(1)} %broadcast_multiply_fusion.5) | copy-start | bytes 3076
  10.0 29.2 %copy-start.39 = (f32[256]{0:T(256)}, f32[256]{0:T(256)S(1)}, u32[]{:S(2)}) copy-start(f32[256]{0:T(256)S(1)} %add_rsqrt_fusion.1) | copy-start | bytes 3076
  12.2 115.5 %reduce-scatter.11.cloned.1.call-start = ((), (), s32[]{:S(2)}) async-start(), calls=%async_computation.9 | async-start | bytes 5898240 | tf_op jit(solution)/shard_map/reduce_scatter | solution.py:104
  12.4 31.6 %copy-start.37 = (f32[288]{0:T(512)}, f32[288]{0:T(512)S(1)}, u32[]{:S(2)}) copy-start(f32[288]{0:T(512)S(1)} %get-tuple-element.296) | copy-start | bytes 3460
  48.8 2.3 copy-start.14
  56.2 2.9 copy-start.5
  56.2 2.9 copy-start.17
  66.4 2.9 copy-start.5
  66.4 2.9 copy-start.17
  73.3 6.4 copy-start.46
  73.4 2.7 copy-start.23
  79.7 48.0 %copy-start.41 = (f32[1152]{0:T(1024)S(1)}, f32[1152]{0:T(1024)}, u32[]{:S(2)}) copy-start(f32[1152]{0:T(1024)} %param.26) | copy-start | bytes 13828
  79.7 50.7 %copy-start.29 = (f32[1152]{0:T(1024)S(1)}, f32[1152]{0:T(1024)}, u32[]{:S(2)}) copy-start(f32[1152]{0:T(1024)} %param.27) | copy-start | bytes 13828
  79.8 50.7 %copy-start.42 = (f32[1152]{0:T(1024)S(1)}, f32[1152]{0:T(1024)}, u32[]{:S(2)}) copy-start(f32[1152]{0:T(1024)} %param.28) | copy-start | bytes 13828
  79.8 94.3 %all-gather.6.cloned.1.call-start = ((), (), s32[]{:S(2)}) async-start(), calls=%async_computation.10 | async-start | bytes 2949120 | tf_op jit(solution)/shard_map/all_gather | solution.py:112
  79.8 51.8 %collective-permute-start = (bf16[256,1152]{1,0:T(8,128)(2,1)}, bf16[256,1152]{1,0:T(8,128)(2,1)}, u32[]{:S(2)}, u32[]{:S(2)}) collective-permute-start(bf16[256,1152]{1,0:T(8,128)(2,1)} %param.33), channel_id=1, source_target_pairs={{0,1},{1,2},{2,3},{3,0},{4,5},{5,6},{6,7},{7,4},{8,9},{9,10},{10,1... | collective-permute-start | bytes 1769480 | tf_op jit(solution)/shard_map/ppermute | solution.py:130
  131.5 112.9 %reduce-scatter.15.cloned.1.call-start = ((), (), s32[]{:S(2)}) async-start(), calls=%async_computation.12 | async-start | bytes 5898240 | tf_op jit(solution)/shard_map/reduce_scatter | solution.py:141
  131.6 9.7 %collective-permute-start.1 = (bf16[256,1152]{1,0:T(8,128)(2,1)}, bf16[256,1152]{1,0:T(8,128)(2,1)}, u32[]{:S(2)}, u32[]{:S(2)}) collective-permute-start(bf16[256,1152]{1,0:T(8,128)(2,1)} %collective-permute-done), channel_id=1, source_target_pairs={{0,1},{1,2},{2,3},{3,0},{4,5},{5,6},{6,7},{7,4},{8,9},{9,10},{10,1... | collective-permute-start | bytes 1769480 | tf_op jit(solution)/shard_map/ppermute | solution.py:130
  141.3 19.4 %collective-permute-start.2 = (bf16[256,1152]{1,0:T(8,128)(2,1)}, bf16[256,1152]{1,0:T(8,128)(2,1)}, u32[]{:S(2)}, u32[]{:S(2)}) collective-permute-start(bf16[256,1152]{1,0:T(8,128)(2,1)} %collective-permute-done.1), channel_id=1, source_target_pairs={{0,1},{1,2},{2,3},{3,0},{4,5},{5,6},{6,7},{7,4},{8,9},{9,10},{10,1... | collective-permute-start | bytes 1769480 | tf_op jit(solution)/shard_map/ppermute | solution.py:130
  141.5 25.0 %copy-start.10 = (bf16[256,1152]{1,0:T(8,128)(2,1)S(1)}, bf16[256,1152]{1,0:T(8,128)(2,1)}, u32[]{:S(2)}) copy-start(bf16[256,1152]{1,0:T(8,128)(2,1)} %param.33) | copy-start | bytes 1769476
  167.3 6.8 copy-start.49
  179.6 10.1 %copy-start.51 = (f32[1024,1076]{0,1:T(8,128)}, f32[1024,1076]{0,1:T(8,128)S(1)}, u32[]{:S(2)}) copy-start(f32[1024,1076]{0,1:T(8,128)S(1)} %convolution_add_fusion) | copy-start | bytes 13221892
  179.6 11.6 %copy-start.48 = (bf16[1152,1076]{0,1:T(8,128)(2,1)S(1)}, bf16[1152,1076]{0,1:T(8,128)(2,1)}, u32[]{:S(2)}) copy-start(bf16[1152,1076]{0,1:T(8,128)(2,1)} %param.29) | copy-start | bytes 7437316
  196.5 83.5 %reduce-scatter.13.cloned.1.call-start = ((), (), s32[]{:S(2)}) async-start(), calls=%async_computation.11 | async-start | bytes 2949120 | tf_op jit(solution)/shard_map/reduce_scatter | solution.py:115
  204.0 40.5 %copy-start.4 = (f32[256,1152]{1,0:T(8,128)S(1)}, f32[256,1152]{1,0:T(8,128)}, u32[]{:S(2)}) copy-start(f32[256,1152]{1,0:T(8,128)} %copy-done.3) | copy-start | bytes 3538948
  204.0 76.0 %copy-start.43 = (f32[1152]{0:T(1024)S(1)}, f32[1152]{0:T(1024)}, u32[]{:S(2)}) copy-start(f32[1152]{0:T(1024)} %param.32) | copy-start | bytes 13828
  204.0 104.8 %all-gather.8.cloned.1.call-start = ((), (), s32[]{:S(2)}) async-start(), calls=%async_computation.13 | async-start | bytes 2949120 | tf_op jit(solution)/shard_map/all_gather | solution.py:150
  283.6 25.2 %copy-start.8 = (f32[256,1152]{1,0:T(8,128)}, f32[256,1152]{1,0:T(8,128)S(1)}, u32[]{:S(2)}) copy-start(f32[256,1152]{1,0:T(8,128)S(1)} %get-tuple-element.340) | copy-start | bytes 3538948
  284.6 173.7 %reduce-scatter.25.cloned.1.call-start = ((), (), s32[]{:S(2)}) async-start(), calls=%async_computation.18 | async-start | bytes 4644864
  312.4 4.0 copy-start.2
  318.2 2.7 copy-start.6
  320.9 3.3 copy-start.20
  324.2 2.4 copy-start.11
  331.0 2.7 copy-start.6
  333.6 3.3 copy-start.20
  337.0 2.4 copy-start.11
  342.3 2.5 copy-start.21
  342.4 8.8 %copy-start.24 = (bf16[1024,4,72]{0,2,1:T(8,128)(2,1)}, bf16[1024,4,72]{0,2,1:T(8,128)(2,1)S(1)}, u32[]{:S(2)}) copy-start(bf16[1024,4,72]{0,2,1:T(8,128)(2,1)S(1)} %convert_element_type.109) | copy-start | bytes 1769476
  344.7 6.5 copy-start.26
  344.9 6.3 copy-start.27
  368.7 1.6 copy-start.22
  368.7 1.7 copy-start.25
  368.8 138.9 %reduce-scatter.17.cloned.1.call-start = ((), (), s32[]{:S(2)}) async-start(), calls=%async_computation.14 | async-start | bytes 5898240 | tf_op jit(solution)/shard_map/reduce_scatter | solution.py:218
  376.8 240.7 %reduce-scatter.23.cloned.1.call-start = ((), (), s32[]{:S(2)}) async-start(), calls=%async_computation.17 | async-start | bytes 5971968 | tf_op jit(solution)/shard_map/reduce_scatter | solution.py:231
  385.5 339.9 %reduce-scatter.21.cloned.1.call-start = ((), (), s32[]{:S(2)}) async-start(), calls=%async_computation.16 | async-start | bytes 5971968 | tf_op jit(solution)/shard_map/reduce_scatter | solution.py:230
  393.8 5.6 copy-start.47
  393.8 27.8 %copy-start.38 = (f32[288]{0:T(512)S(1)}, f32[288]{0:T(512)}, u32[]{:S(2)}) copy-start(f32[288]{0:T(512)} %copy-done.37) | copy-start | bytes 3460
  393.8 401.7 %reduce-scatter.19.cloned.1.call-start = ((), (), s32[]{:S(2)}) async-start(), calls=%async_computation.15 | async-start | bytes 1990656 | tf_op jit(solution)/shard_map/reduce_scatter | solution.py:229
  399.3 24.2 %copy-start.32 = (f32[1152]{0:T(1024)S(1)}, f32[1152]{0:T(1024)}, u32[]{:S(2)}) copy-start(f32[1152]{0:T(1024)} %get-tuple-element.287) | copy-start | bytes 13828
  399.3 24.3 %copy-start.34 = (f32[1152]{0:T(1024)S(1)}, f32[1152]{0:T(1024)}, u32[]{:S(2)}) copy-start(f32[1152]{0:T(1024)} %get-tuple-element.339) | copy-start | bytes 13828
  399.3 24.3 %copy-start.33 = (f32[1152]{0:T(1024)S(1)}, f32[1152]{0:T(1024)}, u32[]{:S(2)}) copy-start(f32[1152]{0:T(1024)} %get-tuple-element.352) | copy-start | bytes 13828
  399.4 24.3 %copy-start.31 = (f32[1152]{0:T(1024)S(1)}, f32[1152]{0:T(1024)}, u32[]{:S(2)}) copy-start(f32[1152]{0:T(1024)} %get-tuple-element.293) | copy-start | bytes 13828
  399.4 24.3 %copy-start.13 = (bf16[2,512,4,72]{1,3,2,0:T(8,128)(2,1)S(1)}, bf16[2,512,4,72]{1,3,2,0:T(8,128)(2,1)}, u32[]{:S(2)}) copy-start(bf16[2,512,4,72]{1,3,2,0:T(8,128)(2,1)} %get-tuple-element.176) | copy-start | bytes 1769476
  399.4 24.7 %copy-start.44 = (f32[1076]{0:T(1024)S(1)}, f32[1076]{0:T(1024)}, u32[]{:S(2)}) copy-start(f32[1076]{0:T(1024)} %get-tuple-element.353) | copy-start | bytes 12916
  421.5 39.3 %copy-start.50 = (f32[4]{0:T(128)}, f32[4]{0:T(128)S(1)}, u32[]{:S(2)}) copy-start(f32[4]{0:T(128)S(1)} %pmax.7) | copy-start | bytes 52
  423.6 84.1 %copy-start.7 = (bf16[256,1152]{1,0:T(8,128)(2,1)S(1)}, bf16[256,1152]{1,0:T(8,128)(2,1)}, u32[]{:S(2)}) copy-start(bf16[256,1152]{1,0:T(8,128)(2,1)} %param.19) | copy-start | bytes 1769476
  423.6 84.1 %copy-start.30 = (f32[1152]{0:T(1024)S(1)}, f32[1152]{0:T(1024)}, u32[]{:S(2)}) copy-start(f32[1152]{0:T(1024)} %param.21) | copy-start | bytes 13828
  423.6 84.1 %copy-start.36 = (f32[256]{0:T(256)S(1)}, f32[256]{0:T(256)}, u32[]{:S(2)}) copy-start(f32[256]{0:T(256)} %copy-done.35) | copy-start | bytes 3076
  423.6 84.1 %copy-start.40 = (f32[256]{0:T(256)S(1)}, f32[256]{0:T(256)}, u32[]{:S(2)}) copy-start(f32[256]{0:T(256)} %copy-done.39) | copy-start | bytes 3076
  460.7 334.8 %copy-start.1 = (bf16[1076,1152]{1,0:T(8,128)(2,1)S(1)}, bf16[1076,1152]{1,0:T(8,128)(2,1)}, u32[]{:S(2)}) copy-start(bf16[1076,1152]{1,0:T(8,128)(2,1)} %param.31) | copy-start | bytes 7437316
  (12 other events, 13.6 us)
Sparse Core Ops, SparseCore 0:
  12.4 26.7 all-gather.3
  79.9 47.8 reduce-scatter.10
  131.7 28.9 all-gather.5
  196.6 47.8 reduce-scatter.14
  246.8 33.0 reduce-scatter.12
  284.7 24.0 all-gather.7
  368.9 88.4 reduce-scatter.24
  459.9 47.7 reduce-scatter.16
  512.2 105.1 reduce-scatter.22
  621.5 103.9 reduce-scatter.20
  729.9 65.6 reduce-scatter.18
